TPU v7x, 32 devices: a whole 2x2x4 slice. The times are simulated.
32 devices in a mesh: tile: 8 (over y, x, core), lev: 4 (over z).
Axes of the slice: x: 2, y: 2, z: 4, core: 2. Of those that a mesh axis runs over, the one named last changes fastest.
Arguments:
- conc: float32 [8, 4, 16, 4, 4096], P('tile', None, None, 'lev'), may hold values from 0 to 2
- wind_u: float32 [8, 4, 4096], P('tile', 'lev'), may hold values from 0.02 to 0.2
- wind_v: float32 [8, 4, 4096], P('tile', 'lev'), may hold values from 0.02 to 0.2
- emission: float32 [8, 4096], P('tile'), may hold values from 0.01 to 1
- member_rate: float32 [4, 16], replicated, may hold values from 0.1 to 2
- column_top: int32 [4], replicated, may hold values from 1 to 4
- settle_rate: float32 [16, 4], replicated, may hold values from 0.5 to 30
- neighbours: int32 [8, 4], replicated, may hold values from -1 to 7, as said below
Outputs:
- final_conc: float32 [8, 4, 16, 4, 4096], P('tile', None, None, 'lev')
Inputs may be any that keep to these rules, and one draw needn't show every extreme that they name: Tiles form a grid 8 tiles wide; each tile's entries name its grid neighbours, and a tile named as some tile's east neighbour names that tile as its west neighbour (likewise south and north).
All inputs are finite; a program needn't handle non-finite values.
Results may differ from a plain program's by a relative error of at most 0.0001.
Values sent between devices are 32-bit elements; how exact they have to be, the bound alone decides.
A program may use at most 64 MiB of HBM per device.

v0:
```python
import functools
import jax
import jax.numpy as jnp
from jax import lax
from jax.experimental import pallas as pl
from jax.experimental.pallas import tpu as pltpu
from jax.sharding import PartitionSpec as P

TS = 64
STEPS = 6


def make_inverse(settle_rate):
    levels = settle_rate.shape[1]
    ident = jnp.eye(levels, dtype=settle_rate.dtype)
    diag_all = 1.0 + settle_rate
    next_rate = jnp.concatenate([settle_rate[:, 1:], jnp.zeros_like(settle_rate[:, :1])], axis=1)

    def back_step(carry, inputs):
        unit_row, rate_next, diag_here = inputs
        row_now = (unit_row[None, :] + rate_next[:, None] * carry) / diag_here[:, None]
        return (row_now, row_now)

    start = jnp.zeros((settle_rate.shape[0], levels), dtype=settle_rate.dtype)
    unused, stacked = lax.scan(back_step, start, (ident, next_rate.T, diag_all.T), reverse=True)
    return jnp.transpose(stacked, (1, 0, 2))


def pick_face(all_faces, index, which):
    chosen = all_faces[jnp.clip(index, 0, all_faces.shape[0] - 1), which]
    valid = (index >= 0).astype(jnp.float32)
    return chosen * valid[:, None, None, None, None]


def horizontal(field, speed_u, speed_v, own_lists):
    per_tile, members, bins, levels, cells = field.shape
    side = TS
    west_face = field[..., 0::side]
    east_face = field[..., side - 1 :: side]
    south_face = field[..., :side]
    north_face = field[..., cells - side :]
    edge_stack = jnp.stack([west_face, east_face, south_face, north_face], axis=1)
    edge_flat = edge_stack.reshape(per_tile, 4, members, bins, levels * side)
    gathered = lax.all_gather(edge_flat, "tile", axis=0, tiled=True)
    all_faces = gathered.reshape(gathered.shape[0], 4, members, bins, levels, side)
    ghost_west = pick_face(all_faces, own_lists[:, 0], 1)
    ghost_east = pick_face(all_faces, own_lists[:, 1], 0)
    ghost_south = pick_face(all_faces, own_lists[:, 2], 3)
    ghost_north = pick_face(all_faces, own_lists[:, 3], 2)
    column_of = jnp.arange(cells, dtype=jnp.int32) % side
    shifted_right = jnp.concatenate([field[..., :1], field[..., :-1]], axis=-1)
    shifted_left = jnp.concatenate([field[..., 1:], field[..., -1:]], axis=-1)
    from_west = jnp.where(column_of == 0, jnp.repeat(ghost_west, side, axis=-1), shifted_right)
    from_east = jnp.where(
        column_of == side - 1, jnp.repeat(ghost_east, side, axis=-1), shifted_left
    )
    from_south = jnp.concatenate([ghost_south, field[..., : cells - side]], axis=-1)
    from_north = jnp.concatenate([field[..., side:], ghost_north], axis=-1)
    moved = field + 0.15 * (from_west + from_east + from_south + from_north - 4.0 * field)
    moved = moved - speed_u * (field - from_west) - speed_v * (field - from_south)
    return moved


def per_device(conc, wind_u, wind_v, emission, member_rate, column_top, settle_rate, neighbours):
    per_tile, members, bins, level_count, cells = conc.shape
    own_lists = lax.dynamic_slice_in_dim(neighbours, lax.axis_index("tile") * per_tile, per_tile, 0)
    inverse = make_inverse(settle_rate)
    levels_here = lax.axis_index("lev") * level_count + jnp.arange(level_count, dtype=jnp.int32)
    below = (levels_here[None, :] < column_top[:, None]).astype(jnp.float32)
    source = (
        emission[:, None, None, None, :]
        * member_rate[None, :, :, None, None]
        * below[None, :, None, :, None]
    )
    speed_u = wind_u.reshape(per_tile, 1, 1, level_count, cells)
    speed_v = wind_v.reshape(per_tile, 1, 1, level_count, cells)
    field = conc
    for turn_index in range(STEPS):
        field = field + source
        moved = horizontal(field, speed_u, speed_v, own_lists)
        columns = lax.all_to_all(moved, "lev", split_axis=4, concat_axis=3, tiled=True)
        settled = jnp.einsum("bkj,tmbjc->tmbkc", inverse, columns, precision=lax.Precision.HIGHEST)
        field = lax.all_to_all(settled, "lev", split_axis=3, concat_axis=4, tiled=True)
    return field


GRID_WIDTH = 8
HALO = 8
GROUP = 4


def lane_of(shape):
    return lax.broadcasted_iota(jnp.int32, shape, 1)


def pack_edges(tiles):
    group = ((lane_of(tiles[0].shape) + HALO) // (2 * HALO)) % GROUP
    packed = tiles[0]
    for i in range(1, len(tiles)):
        packed = jnp.where(group == i, pltpu.roll(tiles[i], 2 * HALO * i, 1), packed)
    return packed


def spread(main, edges, i):
    own = lane_of(main.shape) < TS
    turned = edges if i == 0 else pltpu.roll(edges, 128 - 2 * HALO * i, 1)
    even = jnp.where(own, main, pltpu.roll(turned, TS, 1))
    odd = jnp.where(own, pltpu.roll(main, TS, 1), turned)
    return even, odd


def window_kernel(
    tiles, levs, members,
    rate_ref, top_ref, settle_ref, near_ref, x_ref, u_ref, v_ref, em_ref,
    out_ref,
    inbuf, wind, em, halo, whalo, pick, eo, coef, emx, outbuf, solve,
    in_send, in_recv, wind_send, wind_recv, em_sem, whalo_send, whalo_recv, halo_send, halo_recv, out_send, out_recv,
):
    t = lax.axis_index("tile")
    d = lax.axis_index("lev")
    lev_peers = [lax.rem(d + o, levs) for o in range(1, levs)]
    tile_peers = [lax.rem(t + o, tiles) for o in range(1, tiles)]
    shape = (TS // 2, 128)

    barrier = pltpu.get_barrier_semaphore()
    for p in lev_peers:
        pl.semaphore_signal(barrier, inc=1, device_id={"lev": p})
    for p in tile_peers:
        pl.semaphore_signal(barrier, inc=1, device_id={"tile": p})
    pl.semaphore_wait(barrier, len(lev_peers) + len(tile_peers))

    def remote(src, dst, send_sem, recv_sem, where):
        return pltpu.make_async_remote_copy(
            src_ref=src, dst_ref=dst, send_sem=send_sem, recv_sem=recv_sem, device_id=where
        )

    def mine(p):
        return pl.ds(p * GROUP, GROUP)

    def wind_copy(w, p, slot):
        return remote((u_ref, v_ref)[w], wind.at[w, slot], wind_send.at[w, p], wind_recv.at[w, slot], {"lev": p})

    def in_copy(c, p, slot):
        return remote(x_ref.at[c, mine(p)], inbuf.at[c, slot], in_send.at[c, p], in_recv.at[c, slot], {"lev": p})

    def out_copy(c, p, slot):
        return remote(
            outbuf.at[c, p], out_ref.at[c, mine(slot)], out_send.at[c, p], out_recv.at[c, slot], {"lev": p}
        )

    def wind_edge_copy(p, slot):
        return remote(whalo.at[t], whalo.at[slot], whalo_send.at[p], whalo_recv.at[slot], {"tile": p})

    def edge_copy(c, p, slot):
        return remote(halo.at[c, t], halo.at[c, slot], halo_send.at[c, p], halo_recv.at[c, slot], {"tile": p})

    def own_wind(w):
        return pltpu.make_async_copy((u_ref, v_ref)[w], wind.at[w, d], wind_recv.at[w, d])

    def own_in(c):
        return pltpu.make_async_copy(x_ref.at[c, mine(d)], inbuf.at[c, d], in_recv.at[c, d])

    def own_out(c):
        return pltpu.make_async_copy(outbuf.at[c, d], out_ref.at[c, mine(d)], out_recv.at[c, d])

    def start_in(c):
        for p in lev_peers:
            in_copy(c, p, d).start()
        own_in(c).start()

    for w in range(2):
        for p in lev_peers:
            wind_copy(w, p, d).start()
        own_wind(w).start()
    own_em = pltpu.make_async_copy(em_ref, em, em_sem)
    own_em.start()
    start_in(0)
    start_in(1)

    for i in range(GROUP):
        for k in range(levs):
            q = 1.0 / (1.0 + jnp.full((8, 128), settle_ref[k, d * GROUP + i], jnp.float32))
            solve[i, k, 0] = q
            if k + 1 < levs:
                solve[i, k, 1] = q * settle_ref[k + 1, d * GROUP + i]
            else:
                solve[i, k, 1] = jnp.zeros((8, 128), jnp.float32)

    lane = lane_of(shape)
    row = lax.broadcasted_iota(jnp.int32, shape, 0)
    west, east = near_ref[0, t], near_ref[1, t]
    has_west = jnp.where(west >= 0, 1.0, 0.0)
    has_east = jnp.where(east >= 0, 1.0, 0.0)
    east_lane = lax.rem(lane_of((8, 128)), 2 * HALO) < HALO
    for p in range(tiles):
        pick[p] = jnp.where(
            east_lane,
            jnp.full((8, 128), jnp.where(east == p, 1.0, 0.0), jnp.float32),
            jnp.full((8, 128), jnp.where(west == p, 1.0, 0.0), jnp.float32),
        )

    def wide(value):
        return jnp.concatenate([value] * (shape[0] // 8), axis=0)

    def edges_of(packed):
        total = wide(pick[0]) * packed(0)
        for p in range(1, tiles):
            total = total + wide(pick[p]) * packed(p)
        return total

    own_em.wait()
    for w in range(2):
        own_wind(w).wait()
        for p in lev_peers:
            wind_copy(w, p, p).wait_recv()
    for w in range(2):
        whalo[t, w] = pack_edges([wind[w, k] for k in range(levs)])
    whalo[t, 2] = em[...]
    for p in tile_peers:
        wind_edge_copy(p, t).start()

    def gather_edges(c):
        own_in(c).wait()
        for p in lev_peers:
            in_copy(c, p, p).wait_recv()

        @pl.when(c + 2 < members)
        def _():
            start_in(c + 2)

        def pack_level(k, carry):
            halo[c, t, k] = pack_edges([inbuf[c, k, i] for i in range(GROUP)])
            return carry

        lax.fori_loop(0, levs, pack_level, 0)
        for p in tile_peers:
            edge_copy(c, p, t).start()

    def coefficients():
        for p in tile_peers:
            wind_edge_copy(p, p).wait_recv()
        live = jnp.where(lane < TS, 1.0, 0.0)
        live = jnp.where((lane >= TS) & (lane < TS + HALO), has_east, live)
        live = jnp.where(lane >= 128 - HALO, has_west, live)
        edges = [edges_of(lambda p, w=w: whalo[p, w]) for w in range(3)]
        even, odd = spread(em[...], edges[2], 0)
        emx[0] = even * live
        emx[1] = odd * live
        emx[2] = 0.15 * live
        emx[3] = jnp.where(row == TS // 2 - 1, 0.0, 0.15 * live)
        for k in range(levs):
            us = spread(wind[0, k], edges[0], k)
            vs = spread(wind[1, k], edges[1], k)
            for e in range(2):
                coef[k, e, 0] = (0.4 - us[e] - vs[e]) * live
                coef[k, e, 1] = (0.15 + us[e]) * live
                south = (0.15 + vs[e]) * live
                coef[k, e, 2] = jnp.where(row == 0, 0.0, south) if e == 0 else south

    def run(c):
        for p in tile_peers:
            edge_copy(c, p, p).wait_recv()

        def build(k, carry):
            edges = edges_of(lambda p: halo[c, p, k])
            for i in range(GROUP):
                even, odd = spread(inbuf[c, k, i], edges, i)
                eo[k, i, 0] = even
                eo[k, i, 1] = odd
            return carry

        lax.fori_loop(0, levs, build, 0)

        def one_bin(i, carry):
            rate = rate_ref[c, d * GROUP + i]
            above_even = above_odd = None
            for k in reversed(range(levs)):
                s = jnp.where(k < top_ref[c], rate, 0.0)
                even = eo[k, i, 0] + emx[0] * s
                odd = eo[k, i, 1] + emx[1] * s
                moved_even = (
                    coef[k, 0, 0] * even
                    + coef[k, 0, 1] * pltpu.roll(even, 1, 1)
                    + coef[k, 0, 2] * pltpu.roll(odd, 1, 0)
                    + emx[2] * (pltpu.roll(even, 127, 1) + odd)
                )
                moved_odd = (
                    coef[k, 1, 0] * odd
                    + coef[k, 1, 1] * pltpu.roll(odd, 1, 1)
                    + coef[k, 1, 2] * even
                    + emx[2] * pltpu.roll(odd, 127, 1)
                    + emx[3] * pltpu.roll(even, shape[0] - 1, 0)
                )
                q = wide(solve[i, k, 0])
                new_even, new_odd = q * moved_even, q * moved_odd
                if above_even is not None:
                    g = wide(solve[i, k, 1])
                    new_even = new_even + g * above_even
                    new_odd = new_odd + g * above_odd
                eo[k, i, 0] = new_even
                eo[k, i, 1] = new_odd
                above_even, above_odd = new_even, new_odd
            return carry

        def one_step(step, carry):
            return lax.fori_loop(0, GROUP, one_bin, carry, unroll=2)

        lax.fori_loop(0, STEPS, one_step, 0)

        def join(k, carry):
            for i in range(GROUP):
                outbuf[c, k, i] = jnp.where(lane < TS, eo[k, i, 0], pltpu.roll(eo[k, i, 1], TS, 1))
            return carry

        lax.fori_loop(0, levs, join, 0)
        for p in lev_peers:
            out_copy(c, p, d).start()
        own_out(c).start()

    gather_edges(0)
    coefficients()

    def one_member(c, carry):
        @pl.when(c + 1 < members)
        def _():
            gather_edges(c + 1)

        run(c)
        return carry

    lax.fori_loop(0, members, one_member, 0)

    def finish(c, carry):
        own_out(c).wait()
        for p in lev_peers:
            out_copy(c, p, p).wait_recv()
            out_copy(c, p, d).wait_send()
            in_copy(c, p, d).wait_send()
        for p in tile_peers:
            edge_copy(c, p, t).wait_send()
        return carry

    for w in range(2):
        for p in lev_peers:
            wind_copy(w, p, d).wait_send()
    for p in tile_peers:
        wind_edge_copy(p, t).wait_send()
    lax.fori_loop(0, members, finish, 0)


def window(tiles, levs, conc, wind_u, wind_v, emission, member_rate, column_top, settle_rate, neighbours):
    members, bins = conc.shape[1], conc.shape[2]
    tile = (TS // 2, 128)
    x = conc.reshape((members, bins) + tile)
    f32 = jnp.float32
    dma = pltpu.SemaphoreType.DMA
    smem = pl.BlockSpec(memory_space=pltpu.SMEM)
    hbm = pl.BlockSpec(memory_space=pltpu.HBM)
    anywhere = pl.BlockSpec(memory_space=pl.ANY)
    out = pl.pallas_call(
        functools.partial(window_kernel, tiles, levs, members),
        out_shape=pltpu.VMEM(x.shape, f32),
        in_specs=[smem] * 4 + [hbm] * 4,
        out_specs=pl.BlockSpec(memory_space=pltpu.VMEM),
        scratch_shapes=[
            pltpu.VMEM((members, levs, GROUP) + tile, f32),
            pltpu.VMEM((2, levs) + tile, f32),
            pltpu.VMEM(tile, f32),
            pltpu.VMEM((members, tiles, levs) + tile, f32),
            pltpu.VMEM((tiles, 3) + tile, f32),
            pltpu.VMEM((tiles, 8, 128), f32),
            pltpu.VMEM((levs, GROUP, 2) + tile, f32),
            pltpu.VMEM((levs, 2, 3) + tile, f32),
            pltpu.VMEM((4,) + tile, f32),
            pltpu.VMEM((members, levs, GROUP) + tile, f32),
            pltpu.VMEM((GROUP, levs, 2, 8, 128), f32),
            dma((members, levs)),
            dma((members, levs)),
            dma((2, levs)),
            dma((2, levs)),
            dma,
            dma((tiles,)),
            dma((tiles,)),
            dma((members, tiles)),
            dma((members, tiles)),
            dma((members, levs)),
            dma((members, levs)),
        ],
        compiler_params=pltpu.CompilerParams(
            collective_id=0, has_side_effects=True, vmem_limit_bytes=58 * 1024 * 1024
        ),
        name="window",
    )(
        member_rate, column_top, settle_rate.T, neighbours.T,
        x, wind_u.reshape(tile), wind_v.reshape(tile), emission.reshape(tile),
    )
    return out.reshape(conc.shape)


def choose(mesh):
    tiles, levs = mesh.shape["tile"], mesh.shape["lev"]

    def body(conc, *rest):
        per_tile, members, bins, level_count, cells = conc.shape
        one_row = tiles * per_tile == GRID_WIDTH
        fits = per_tile == 1 and level_count == 1 and bins == levs * GROUP and levs <= GROUP and members > 1
        if one_row and fits and cells == TS * TS and TS == 64 and STEPS <= HALO:
            return window(tiles, levs, conc, *rest)
        return per_device(conc, *rest)

    return body


def solution(mesh):
    return jax.shard_map(
        choose(mesh),
        mesh=mesh,
        in_specs=(
            P("tile", None, None, "lev", None),
            P("tile", "lev", None),
            P("tile", "lev", None),
            P("tile", None),
            P(),
            P(),
            P(),
            P(),
        ),
        out_specs=P("tile", None, None, "lev", None),
        check_vma=False,
    )
```

profile of v0, /device:TPU:1, one launch (start us, length us, event | category | flops | bytes accessed | tf_op | source)
XLA Modules:
  0.0 56.9 jit_solution(12320729657083136631)
XLA Ops:
  0.0 55.9 %window.1 = f32[4,16,32,128]{3,2,1,0:T(8,128)S(1)} custom-call(f32[4,16]{1,0:T(4,128)} %rate_ref.1, s32[4]{0:T(128)} %top_ref.1, f32[4,16]{1,0:T(4,128)} %bitcast.12, s32[4,8]{1,0:T(4,128)} %bitcast.13, f32[4,16,32,128]{3,2,1,0:T(8,128)} %bitcast.8, f32[32,128]{1,0:T(8,128)} %bitcast.9, f32[32,128]{1,0:T(8,128)} %bitcast.10, f32[32,128]{1,0:T(8,128)} %bitcast.11), custom_call_target="tpu_custom_call" | custom-call | tf_op jit(solution)/shard_map/window/pallas_call | solution.py:360
  55.9 1.0 %copy.11 = f32[1,4,16,1,4096]{4,3,2,1,0:T(1,128)} copy(f32[1,4,16,1,4096]{4,3,2,1,0:T(1,128)S(1)} %bitcast.7) | data formatting | bytes 2097152
where the time goes:
time: 57.2 us; the launch traced here: 56.9 us
  Pallas kernels  55.9 us (98%)
  local copies, waits for them, and re-layouts  0.97 us (2%)
    pallas_call x1, Pallas kernels, window(): pl.pallas_call(functools.partial(window_kernel, tiles, levs, members), ou...  55.9 us

commit v1 on v0

--- a/solution.py
+++ b/solution.py
@@ -111,10 +111,12 @@
 
 def window_kernel(
     tiles, levs, members,
-    rate_ref, top_ref, settle_ref, near_ref, x_ref, u_ref, v_ref, em_ref,
+    rate_hbm, top_hbm, settle_hbm, near_hbm, x_ref, u_ref, v_ref, em_ref,
     out_ref,
-    inbuf, wind, em, halo, whalo, pick, eo, coef, emx, outbuf, solve,
-    in_send, in_recv, wind_send, wind_recv, em_sem, whalo_send, whalo_recv, halo_send, halo_recv, out_send, out_recv,
+    rate_ref, top_ref, settle_ref, near_ref,
+    inbuf, wind, halo, whalo, pick, eo, coef, emx, outbuf, solve,
+    in_send, in_recv, near_recv, far_recv, wind_send, relay_send, em_send, em_recv, small_sem,
+    whalo_send, whalo_recv, halo_send, halo_recv, out_send, out_recv, lev_ready, tile_ready,
 ):
     t = lax.axis_index("tile")
     d = lax.axis_index("lev")
@@ -122,12 +124,39 @@
     tile_peers = [lax.rem(t + o, tiles) for o in range(1, tiles)]
     shape = (TS // 2, 128)
 
+    half = levs // 2
+    upper = d >= half
+
     barrier = pltpu.get_barrier_semaphore()
-    for p in lev_peers:
-        pl.semaphore_signal(barrier, inc=1, device_id={"lev": p})
-    for p in tile_peers:
-        pl.semaphore_signal(barrier, inc=1, device_id={"tile": p})
-    pl.semaphore_wait(barrier, len(lev_peers) + len(tile_peers))
+    for p in range(1, levs):
+        @pl.when(d < p)
+        def _():
+            pl.semaphore_signal(barrier, inc=1, device_id={"lev": p})
+    for p in range(1, tiles):
+        @pl.when(t < p)
+        def _():
+            pl.semaphore_signal(barrier, inc=1, device_id={"tile": p})
+    own_small = [
+        pltpu.make_async_copy(src, dst, small_sem.at[i])
+        for i, (src, dst) in enumerate(
+            ((rate_hbm, rate_ref), (top_hbm, top_ref), (settle_hbm, settle_ref), (near_hbm, near_ref))
+        )
+    ]
+    for copy in own_small:
+        copy.start()
+
+    @pl.when(d + t > 0)
+    def _():
+        pl.semaphore_wait(barrier, d + t)
+
+    for p in range(levs - 1):
+        @pl.when(p < d)
+        def _():
+            pl.semaphore_signal(lev_ready.at[d], inc=1, device_id={"lev": p})
+    for p in range(tiles - 1):
+        @pl.when(p < t)
+        def _():
+            pl.semaphore_signal(tile_ready, inc=1, device_id={"tile": p})
 
     def remote(src, dst, send_sem, recv_sem, where):
         return pltpu.make_async_remote_copy(
@@ -137,45 +166,104 @@
     def mine(p):
         return pl.ds(p * GROUP, GROUP)
 
-    def wind_copy(w, p, slot):
-        return remote((u_ref, v_ref)[w], wind.at[w, slot], wind_send.at[w, p], wind_recv.at[w, slot], {"lev": p})
-
-    def in_copy(c, p, slot):
-        return remote(x_ref.at[c, mine(p)], inbuf.at[c, slot], in_send.at[c, p], in_recv.at[c, slot], {"lev": p})
-
-    def out_copy(c, p, slot):
-        return remote(
-            outbuf.at[c, p], out_ref.at[c, mine(slot)], out_send.at[c, p], out_recv.at[c, slot], {"lev": p}
-        )
-
-    def wind_edge_copy(p, slot):
-        return remote(whalo.at[t], whalo.at[slot], whalo_send.at[p], whalo_recv.at[slot], {"tile": p})
-
-    def edge_copy(c, p, slot):
-        return remote(halo.at[c, t], halo.at[c, slot], halo_send.at[c, p], halo_recv.at[c, slot], {"tile": p})
-
-    def own_wind(w):
-        return pltpu.make_async_copy((u_ref, v_ref)[w], wind.at[w, d], wind_recv.at[w, d])
+    def arrived(ref, sem):
+        pltpu.make_async_copy(ref, ref, sem).wait()
+
+    def wind_copy(w, p, sem):
+        return remote((u_ref, v_ref)[w], wind.at[d, w], wind_send, sem, {"lev": p})
+
+    def send_winds(p):
+        same = (d < half) if p < half else upper
+        for w in range(2):
+            @pl.when(same)
+            def _():
+                wind_copy(w, p, near_recv).start()
+            if p in (half - 1, half):
+                @pl.when(jnp.logical_not(same))
+                def _():
+                    wind_copy(w, p, far_recv).start()
+
+    def in_copy(c, p):
+        return remote(x_ref.at[c, mine(p)], inbuf.at[c, d], in_send, in_recv.at[c], {"lev": p})
+
+    def out_copy(c, p):
+        return remote(outbuf.at[c, p], out_ref.at[c, mine(d)], out_send, out_recv, {"lev": p})
+
+    def wind_edge_copy(p):
+        mine_now = whalo.at[t, pl.ds(0, 2)]
+        return remote(mine_now, mine_now, whalo_send, whalo_recv, {"tile": p})
+
+    def em_copy(p):
+        return remote(em_ref, whalo.at[t, 2], em_send, em_recv, {"tile": p})
+
+    def edge_copy(c, p):
+        return remote(halo.at[c, t], halo.at[c, t], halo_send, halo_recv.at[c], {"tile": p})
 
     def own_in(c):
-        return pltpu.make_async_copy(x_ref.at[c, mine(d)], inbuf.at[c, d], in_recv.at[c, d])
+        return pltpu.make_async_copy(x_ref.at[c, mine(d)], inbuf.at[c, d], in_recv.at[c])
 
     def own_out(c):
-        return pltpu.make_async_copy(outbuf.at[c, d], out_ref.at[c, mine(d)], out_recv.at[c, d])
+        return pltpu.make_async_copy(outbuf.at[c, d], out_ref.at[c, mine(d)], out_recv)
 
     def start_in(c):
         for p in lev_peers:
-            in_copy(c, p, d).start()
+            in_copy(c, p).start()
         own_in(c).start()
 
+    for p in reversed(range(levs - 1)):
+        @pl.when(p < d)
+        def _():
+            send_winds(p)
+    for p in range(half):
+        @pl.when(upper)
+        def _():
+            in_copy(0, p).start()
     for w in range(2):
-        for p in lev_peers:
-            wind_copy(w, p, d).start()
-        own_wind(w).start()
-    own_em = pltpu.make_async_copy(em_ref, em, em_sem)
-    own_em.start()
-    start_in(0)
+        pltpu.make_async_copy((u_ref, v_ref)[w], wind.at[d, w], near_recv).start()
+    pltpu.make_async_copy(em_ref, whalo.at[t, 2], em_recv).start()
+    for p in range(1, levs):
+        @pl.when(p > d)
+        def _():
+            pl.semaphore_wait(lev_ready.at[p], 1)
+            send_winds(p)
+            if p >= half:
+                @pl.when(jnp.logical_not(upper))
+                def _():
+                    in_copy(0, p).start()
+
+    @pl.when(t < tiles - 1)
+    def _():
+        pl.semaphore_wait(tile_ready, tiles - 1 - t)
+
+    for p in tile_peers:
+        em_copy(p).start()
+    gates = ((half - 1, range(half - 1), half), (half, range(half + 1, levs), 0))
+    for gate, others, first in gates:
+        @pl.when(d == gate)
+        def _():
+            far = wind.at[pl.ds(first, half)]
+            arrived(far, far_recv)
+            for p in others:
+                remote(far, far, relay_send, far_recv, {"lev": p}).start()
+    for p in range(levs):
+        @pl.when((p != d) & ((p >= half) == upper))
+        def _():
+            in_copy(0, p).start()
+    own_in(0).start()
+    arrived(wind.at[pl.ds(0, half)], near_recv)
+
+    @pl.when((d != half) & (d != half - 1))
+    def _():
+        arrived(wind.at[pl.ds(0, half)], far_recv)
+
+    for w in range(2):
+        whalo[t, w] = pack_edges([wind[k, w] for k in range(levs)])
+    for p in tile_peers:
+        wind_edge_copy(p).start()
     start_in(1)
+
+    for copy in own_small:
+        copy.wait()
 
     for i in range(GROUP):
         for k in range(levs):
@@ -208,21 +296,8 @@
             total = total + wide(pick[p]) * packed(p)
         return total
 
-    own_em.wait()
-    for w in range(2):
-        own_wind(w).wait()
-        for p in lev_peers:
-            wind_copy(w, p, p).wait_recv()
-    for w in range(2):
-        whalo[t, w] = pack_edges([wind[w, k] for k in range(levs)])
-    whalo[t, 2] = em[...]
-    for p in tile_peers:
-        wind_edge_copy(p, t).start()
-
     def gather_edges(c):
-        own_in(c).wait()
-        for p in lev_peers:
-            in_copy(c, p, p).wait_recv()
+        arrived(inbuf.at[c], in_recv.at[c])
 
         @pl.when(c + 2 < members)
         def _():
@@ -234,23 +309,23 @@
 
         lax.fori_loop(0, levs, pack_level, 0)
         for p in tile_peers:
-            edge_copy(c, p, t).start()
+            edge_copy(c, p).start()
 
     def coefficients():
-        for p in tile_peers:
-            wind_edge_copy(p, p).wait_recv()
+        arrived(whalo.at[pl.ds(0, tiles - 1), pl.ds(0, 2)], whalo_recv)
+        arrived(whalo.at[:, 2], em_recv)
         live = jnp.where(lane < TS, 1.0, 0.0)
         live = jnp.where((lane >= TS) & (lane < TS + HALO), has_east, live)
         live = jnp.where(lane >= 128 - HALO, has_west, live)
         edges = [edges_of(lambda p, w=w: whalo[p, w]) for w in range(3)]
-        even, odd = spread(em[...], edges[2], 0)
+        even, odd = spread(whalo[t, 2], edges[2], 0)
         emx[0] = even * live
         emx[1] = odd * live
         emx[2] = 0.15 * live
         emx[3] = jnp.where(row == TS // 2 - 1, 0.0, 0.15 * live)
         for k in range(levs):
-            us = spread(wind[0, k], edges[0], k)
-            vs = spread(wind[1, k], edges[1], k)
+            us = spread(wind[k, 0], edges[0], k)
+            vs = spread(wind[k, 1], edges[1], k)
             for e in range(2):
                 coef[k, e, 0] = (0.4 - us[e] - vs[e]) * live
                 coef[k, e, 1] = (0.15 + us[e]) * live
@@ -258,8 +333,7 @@
                 coef[k, e, 2] = jnp.where(row == 0, 0.0, south) if e == 0 else south
 
     def run(c):
-        for p in tile_peers:
-            edge_copy(c, p, p).wait_recv()
+        arrived(halo.at[c, pl.ds(0, tiles - 1)], halo_recv.at[c])
 
         def build(k, carry):
             edges = edges_of(lambda p: halo[c, p, k])
@@ -314,7 +388,7 @@
 
         lax.fori_loop(0, levs, join, 0)
         for p in lev_peers:
-            out_copy(c, p, d).start()
+            out_copy(c, p).start()
         own_out(c).start()
 
     gather_edges(0)
@@ -330,22 +404,18 @@
 
     lax.fori_loop(0, members, one_member, 0)
 
-    def finish(c, carry):
-        own_out(c).wait()
-        for p in lev_peers:
-            out_copy(c, p, p).wait_recv()
-            out_copy(c, p, d).wait_send()
-            in_copy(c, p, d).wait_send()
-        for p in tile_peers:
-            edge_copy(c, p, t).wait_send()
-        return carry
-
-    for w in range(2):
-        for p in lev_peers:
-            wind_copy(w, p, d).wait_send()
-    for p in tile_peers:
-        wind_edge_copy(p, t).wait_send()
-    lax.fori_loop(0, members, finish, 0)
+    arrived(out_ref, out_recv)
+    arrived(inbuf.at[:, pl.ds(0, levs - 1)], in_send)
+    arrived(wind.at[pl.ds(0, half)], wind_send)
+    for gate, others, first in gates:
+        @pl.when(d == gate)
+        def _():
+            for p in others:
+                arrived(wind.at[pl.ds(0, half)], relay_send)
+    arrived(whalo.at[pl.ds(0, tiles - 1), pl.ds(0, 2)], whalo_send)
+    arrived(whalo.at[pl.ds(0, tiles - 1), 2], em_send)
+    arrived(halo.at[:, pl.ds(0, tiles - 1)], halo_send)
+    arrived(outbuf.at[:, pl.ds(0, levs - 1)], out_send)
 
 
 def window(tiles, levs, conc, wind_u, wind_v, emission, member_rate, column_top, settle_rate, neighbours):
@@ -354,18 +424,19 @@
     x = conc.reshape((members, bins) + tile)
     f32 = jnp.float32
     dma = pltpu.SemaphoreType.DMA
-    smem = pl.BlockSpec(memory_space=pltpu.SMEM)
     hbm = pl.BlockSpec(memory_space=pltpu.HBM)
-    anywhere = pl.BlockSpec(memory_space=pl.ANY)
     out = pl.pallas_call(
         functools.partial(window_kernel, tiles, levs, members),
         out_shape=pltpu.VMEM(x.shape, f32),
-        in_specs=[smem] * 4 + [hbm] * 4,
+        in_specs=[hbm] * 8,
         out_specs=pl.BlockSpec(memory_space=pltpu.VMEM),
         scratch_shapes=[
+            pltpu.SMEM(member_rate.shape, f32),
+            pltpu.SMEM(column_top.shape, jnp.int32),
+            pltpu.SMEM(settle_rate.shape[::-1], f32),
+            pltpu.SMEM(neighbours.shape[::-1], jnp.int32),
             pltpu.VMEM((members, levs, GROUP) + tile, f32),
-            pltpu.VMEM((2, levs) + tile, f32),
-            pltpu.VMEM(tile, f32),
+            pltpu.VMEM((levs, 2) + tile, f32),
             pltpu.VMEM((members, tiles, levs) + tile, f32),
             pltpu.VMEM((tiles, 3) + tile, f32),
             pltpu.VMEM((tiles, 8, 128), f32),
@@ -374,17 +445,23 @@
             pltpu.VMEM((4,) + tile, f32),
             pltpu.VMEM((members, levs, GROUP) + tile, f32),
             pltpu.VMEM((GROUP, levs, 2, 8, 128), f32),
-            dma((members, levs)),
-            dma((members, levs)),
-            dma((2, levs)),
-            dma((2, levs)),
-            dma,
-            dma((tiles,)),
-            dma((tiles,)),
-            dma((members, tiles)),
-            dma((members, tiles)),
-            dma((members, levs)),
-            dma((members, levs)),
+            dma,
+            dma((members,)),
+            dma,
+            dma,
+            dma,
+            dma,
+            dma,
+            dma,
+            dma((4,)),
+            dma,
+            dma,
+            dma,
+            dma((members,)),
+            dma,
+            dma,
+            pltpu.SemaphoreType.REGULAR((levs,)),
+            pltpu.SemaphoreType.REGULAR,
         ],
         compiler_params=pltpu.CompilerParams(
             collective_id=0, has_side_effects=True, vmem_limit_bytes=58 * 1024 * 1024
@@ -403,7 +480,7 @@
     def body(conc, *rest):
         per_tile, members, bins, level_count, cells = conc.shape
         one_row = tiles * per_tile == GRID_WIDTH
-        fits = per_tile == 1 and level_count == 1 and bins == levs * GROUP and levs <= GROUP and members > 1
+        fits = per_tile == 1 and level_count == 1 and bins == levs * GROUP and levs in (2, GROUP) and members > 1
         if one_row and fits and cells == TS * TS and TS == 64 and STEPS <= HALO:
             return window(tiles, levs, conc, *rest)
         return per_device(conc, *rest)

time: 57.2 us -> 52.3 us (0.914)
  Pallas kernels: 55.9 us -> 50.8 us
    pallas_call x1, Pallas kernels: 55.9 us -> 50.8 us  [window(): pl.pallas_call(functools.partial(window_kernel, tiles, levs, members), ou...]
where the time goes in v1:
time: 52.3 us; the launch traced here: 51.8 us
  Pallas kernels  50.8 us (97%)
  local copies, waits for them, and re-layouts  0.97 us (2%)
    pallas_call x1, Pallas kernels, window(): pl.pallas_call(functools.partial(window_kernel, tiles, levs, members), ou...  50.8 us

profile of v1, /device:TPU:1, one launch (start us, length us, event | category | flops | bytes accessed | tf_op | source)
XLA Modules:
  0.0 51.8 jit_solution(13727103351244798533)
XLA Ops:
  0.0 50.8 %window.1 = f32[4,16,32,128]{3,2,1,0:T(8,128)S(1)} custom-call(f32[4,16]{1,0:T(4,128)} %rate_hbm.1, s32[4]{0:T(128)} %top_hbm.1, f32[4,16]{1,0:T(4,128)} %bitcast.12, s32[4,8]{1,0:T(4,128)} %bitcast.13, f32[4,16,32,128]{3,2,1,0:T(8,128)} %bitcast.8, f32[32,128]{1,0:T(8,128)} %bitcast.9, f32[32,128]{1,0:T(8,128)} %bitcast.10, f32[32,128]{1,0:T(8,128)} %bitcast.11), custom_call_target="tpu_custom_call" | custom-call | tf_op jit(solution)/shard_map/window/pallas_call | solution.py:428
  50.8 1.0 %copy.11 = f32[1,4,16,1,4096]{4,3,2,1,0:T(1,128)} copy(f32[1,4,16,1,4096]{4,3,2,1,0:T(1,128)S(1)} %bitcast.7) | data formatting | bytes 2097152

commit v2 on v1

--- a/solution.py
+++ b/solution.py
@@ -132,10 +132,6 @@
         @pl.when(d < p)
         def _():
             pl.semaphore_signal(barrier, inc=1, device_id={"lev": p})
-    for p in range(1, tiles):
-        @pl.when(t < p)
-        def _():
-            pl.semaphore_signal(barrier, inc=1, device_id={"tile": p})
     own_small = [
         pltpu.make_async_copy(src, dst, small_sem.at[i])
         for i, (src, dst) in enumerate(
@@ -145,18 +141,14 @@
     for copy in own_small:
         copy.start()
 
-    @pl.when(d + t > 0)
+    @pl.when(d > 0)
     def _():
-        pl.semaphore_wait(barrier, d + t)
+        pl.semaphore_wait(barrier, d)
 
     for p in range(levs - 1):
         @pl.when(p < d)
         def _():
             pl.semaphore_signal(lev_ready.at[d], inc=1, device_id={"lev": p})
-    for p in range(tiles - 1):
-        @pl.when(p < t)
-        def _():
-            pl.semaphore_signal(tile_ready, inc=1, device_id={"tile": p})
 
     def remote(src, dst, send_sem, recv_sem, where):
         return pltpu.make_async_remote_copy(
@@ -231,12 +223,14 @@
                 def _():
                     in_copy(0, p).start()
 
-    @pl.when(t < tiles - 1)
+    @pl.when(d == 0)
     def _():
-        pl.semaphore_wait(tile_ready, tiles - 1 - t)
-
-    for p in tile_peers:
-        em_copy(p).start()
+        for p in tile_peers:
+            pl.semaphore_signal(barrier, inc=1, device_id={"tile": p})
+        pl.semaphore_wait(barrier, tiles - 1)
+        for p in range(1, levs):
+            pl.semaphore_signal(tile_ready, inc=1, device_id={"lev": p})
+
     gates = ((half - 1, range(half - 1), half), (half, range(half + 1, levs), 0))
     for gate, others, first in gates:
         @pl.when(d == gate)
@@ -256,6 +250,12 @@
     def _():
         arrived(wind.at[pl.ds(0, half)], far_recv)
 
+    @pl.when(d > 0)
+    def _():
+        pl.semaphore_wait(tile_ready, 1)
+
+    for p in tile_peers:
+        em_copy(p).start()
     for w in range(2):
         whalo[t, w] = pack_edges([wind[k, w] for k in range(levs)])
     for p in tile_peers:

time: 52.3 us -> 50.7 us (0.969)
  Pallas kernels: 50.8 us -> 49.1 us
    pallas_call x1, Pallas kernels: 50.8 us -> 49.1 us  [window(): pl.pallas_call(functools.partial(window_kernel, tiles, levs, members), ou...]
where the time goes in v2:
time: 50.7 us; the launch traced here: 50 us
  Pallas kernels  49.1 us (97%)
  local copies, waits for them, and re-layouts  0.97 us (2%)
    pallas_call x1, Pallas kernels, window(): pl.pallas_call(functools.partial(window_kernel, tiles, levs, members), ou...  49.1 us

profile of v2, /device:TPU:1, one launch (start us, length us, event | category | flops | bytes accessed | tf_op | source)
XLA Modules:
  0.0 50.0 jit_solution(15870175675246128347)
XLA Ops:
  0.0 49.1 %window.1 = f32[4,16,32,128]{3,2,1,0:T(8,128)S(1)} custom-call(f32[4,16]{1,0:T(4,128)} %rate_hbm.1, s32[4]{0:T(128)} %top_hbm.1, f32[4,16]{1,0:T(4,128)} %bitcast.12, s32[4,8]{1,0:T(4,128)} %bitcast.13, f32[4,16,32,128]{3,2,1,0:T(8,128)} %bitcast.8, f32[32,128]{1,0:T(8,128)} %bitcast.9, f32[32,128]{1,0:T(8,128)} %bitcast.10, f32[32,128]{1,0:T(8,128)} %bitcast.11), custom_call_target="tpu_custom_call" | custom-call | tf_op jit(solution)/shard_map/window/pallas_call | solution.py:428
  49.1 1.0 %copy.11 = f32[1,4,16,1,4096]{4,3,2,1,0:T(1,128)} copy(f32[1,4,16,1,4096]{4,3,2,1,0:T(1,128)S(1)} %bitcast.7) | data formatting | bytes 2097152

commit v3 on v2

--- a/solution.py
+++ b/solution.py
@@ -115,8 +115,8 @@
     out_ref,
     rate_ref, top_ref, settle_ref, near_ref,
     inbuf, wind, halo, whalo, pick, eo, coef, emx, outbuf, solve,
-    in_send, in_recv, near_recv, far_recv, wind_send, relay_send, em_send, em_recv, small_sem,
-    whalo_send, whalo_recv, halo_send, halo_recv, out_send, out_recv, lev_ready, tile_ready,
+    lev_send, in_recv, near_recv, far_recv, wind_send, small_sem,
+    whalo_send, whalo_recv, halo_send, halo_recv, out_recv, lev_ready, tile_ready,
 ):
     t = lax.axis_index("tile")
     d = lax.axis_index("lev")
@@ -148,7 +148,7 @@
     for p in range(levs - 1):
         @pl.when(p < d)
         def _():
-            pl.semaphore_signal(lev_ready.at[d], inc=1, device_id={"lev": p})
+            pl.semaphore_signal(lev_ready.at[d - 1], inc=1, device_id={"lev": p})
 
     def remote(src, dst, send_sem, recv_sem, where):
         return pltpu.make_async_remote_copy(
@@ -176,17 +176,17 @@
                     wind_copy(w, p, far_recv).start()
 
     def in_copy(c, p):
-        return remote(x_ref.at[c, mine(p)], inbuf.at[c, d], in_send, in_recv.at[c], {"lev": p})
+        return remote(x_ref.at[c, mine(p)], inbuf.at[c, d], lev_send, in_recv.at[c], {"lev": p})
 
     def out_copy(c, p):
-        return remote(outbuf.at[c, p], out_ref.at[c, mine(d)], out_send, out_recv, {"lev": p})
+        return remote(outbuf.at[c, p], out_ref.at[c, mine(d)], lev_send, out_recv, {"lev": p})
 
     def wind_edge_copy(p):
         mine_now = whalo.at[t, pl.ds(0, 2)]
         return remote(mine_now, mine_now, whalo_send, whalo_recv, {"tile": p})
 
     def em_copy(p):
-        return remote(em_ref, whalo.at[t, 2], em_send, em_recv, {"tile": p})
+        return remote(em_ref, whalo.at[t, 2], whalo_send, whalo_recv, {"tile": p})
 
     def edge_copy(c, p):
         return remote(halo.at[c, t], halo.at[c, t], halo_send, halo_recv.at[c], {"tile": p})
@@ -212,11 +212,11 @@
             in_copy(0, p).start()
     for w in range(2):
         pltpu.make_async_copy((u_ref, v_ref)[w], wind.at[d, w], near_recv).start()
-    pltpu.make_async_copy(em_ref, whalo.at[t, 2], em_recv).start()
+    pltpu.make_async_copy(em_ref, whalo.at[t, 2], near_recv).start()
     for p in range(1, levs):
         @pl.when(p > d)
         def _():
-            pl.semaphore_wait(lev_ready.at[p], 1)
+            pl.semaphore_wait(lev_ready.at[p - 1], 1)
             send_winds(p)
             if p >= half:
                 @pl.when(jnp.logical_not(upper))
@@ -238,13 +238,13 @@
             far = wind.at[pl.ds(first, half)]
             arrived(far, far_recv)
             for p in others:
-                remote(far, far, relay_send, far_recv, {"lev": p}).start()
+                remote(far, far, wind_send, far_recv, {"lev": p}).start()
     for p in range(levs):
         @pl.when((p != d) & ((p >= half) == upper))
         def _():
             in_copy(0, p).start()
     own_in(0).start()
-    arrived(wind.at[pl.ds(0, half)], near_recv)
+    arrived(whalo.at[pl.ds(0, 2 * half + 1), 0], near_recv)
 
     @pl.when((d != half) & (d != half - 1))
     def _():
@@ -299,10 +299,6 @@
     def gather_edges(c):
         arrived(inbuf.at[c], in_recv.at[c])
 
-        @pl.when(c + 2 < members)
-        def _():
-            start_in(c + 2)
-
         def pack_level(k, carry):
             halo[c, t, k] = pack_edges([inbuf[c, k, i] for i in range(GROUP)])
             return carry
@@ -312,8 +308,7 @@
             edge_copy(c, p).start()
 
     def coefficients():
-        arrived(whalo.at[pl.ds(0, tiles - 1), pl.ds(0, 2)], whalo_recv)
-        arrived(whalo.at[:, 2], em_recv)
+        arrived(whalo.at[pl.ds(0, tiles - 1)], whalo_recv)
         live = jnp.where(lane < TS, 1.0, 0.0)
         live = jnp.where((lane >= TS) & (lane < TS + HALO), has_east, live)
         live = jnp.where(lane >= 128 - HALO, has_west, live)
@@ -392,7 +387,9 @@
         own_out(c).start()
 
     gather_edges(0)
+    start_in(2)
     coefficients()
+    start_in(3)
 
     def one_member(c, carry):
         @pl.when(c + 1 < members)
@@ -405,17 +402,18 @@
     lax.fori_loop(0, members, one_member, 0)
 
     arrived(out_ref, out_recv)
-    arrived(inbuf.at[:, pl.ds(0, levs - 1)], in_send)
-    arrived(wind.at[pl.ds(0, half)], wind_send)
-    for gate, others, first in gates:
-        @pl.when(d == gate)
-        def _():
-            for p in others:
-                arrived(wind.at[pl.ds(0, half)], relay_send)
-    arrived(whalo.at[pl.ds(0, tiles - 1), pl.ds(0, 2)], whalo_send)
-    arrived(whalo.at[pl.ds(0, tiles - 1), 2], em_send)
+    arrived(halo.at[:, pl.ds(0, 2 * (levs - 1))], lev_send)
+
+    @pl.when((d == half) | (d == half - 1))
+    def _():
+        arrived(wind.at[pl.ds(0, 2 * half)], wind_send)
+
+    @pl.when((d != half) & (d != half - 1))
+    def _():
+        arrived(wind.at[pl.ds(0, half)], wind_send)
+
+    arrived(whalo.at[pl.ds(0, tiles - 1)], whalo_send)
     arrived(halo.at[:, pl.ds(0, tiles - 1)], halo_send)
-    arrived(outbuf.at[:, pl.ds(0, levs - 1)], out_send)
 
 
 def window(tiles, levs, conc, wind_u, wind_v, emission, member_rate, column_top, settle_rate, neighbours):
@@ -450,17 +448,13 @@
             dma,
             dma,
             dma,
-            dma,
-            dma,
-            dma,
             dma((4,)),
             dma,
             dma,
             dma,
             dma((members,)),
             dma,
-            dma,
-            pltpu.SemaphoreType.REGULAR((levs,)),
+            pltpu.SemaphoreType.REGULAR((levs - 1,)),
             pltpu.SemaphoreType.REGULAR,
         ],
         compiler_params=pltpu.CompilerParams(
@@ -480,7 +474,7 @@
     def body(conc, *rest):
         per_tile, members, bins, level_count, cells = conc.shape
         one_row = tiles * per_tile == GRID_WIDTH
-        fits = per_tile == 1 and level_count == 1 and bins == levs * GROUP and levs in (2, GROUP) and members > 1
+        fits = per_tile == 1 and level_count == 1 and bins == levs * GROUP and levs == GROUP and members > 1
         if one_row and fits and cells == TS * TS and TS == 64 and STEPS <= HALO:
             return window(tiles, levs, conc, *rest)
         return per_device(conc, *rest)

time: 50.7 us -> 50.7 us (level)
  no operation moved by 1% of the time
where the time goes in v3:
time: 50.7 us; the launch traced here: 50 us
  Pallas kernels  49 us (97%)
  local copies, waits for them, and re-layouts  0.97 us (2%)
    pallas_call x1, Pallas kernels, window(): pl.pallas_call(functools.partial(window_kernel, tiles, levs, members), ou...  49 us

profile of v3, /device:TPU:1, one launch (start us, length us, event | category | flops | bytes accessed | tf_op | source)
XLA Modules:
  0.0 50.0 jit_solution(18070114767648779442)
XLA Ops:
  0.0 49.0 %window.1 = f32[4,16,32,128]{3,2,1,0:T(8,128)S(1)} custom-call(f32[4,16]{1,0:T(4,128)} %rate_hbm.1, s32[4]{0:T(128)} %top_hbm.1, f32[4,16]{1,0:T(4,128)} %bitcast.12, s32[4,8]{1,0:T(4,128)} %bitcast.13, f32[4,16,32,128]{3,2,1,0:T(8,128)} %bitcast.8, f32[32,128]{1,0:T(8,128)} %bitcast.9, f32[32,128]{1,0:T(8,128)} %bitcast.10, f32[32,128]{1,0:T(8,128)} %bitcast.11), custom_call_target="tpu_custom_call" | custom-call | tf_op jit(solution)/shard_map/window/pallas_call | solution.py:426
  49.0 1.0 %copy.11 = f32[1,4,16,1,4096]{4,3,2,1,0:T(1,128)} copy(f32[1,4,16,1,4096]{4,3,2,1,0:T(1,128)S(1)} %bitcast.7) | data formatting | bytes 2097152

commit v4 on v3

--- a/solution.py
+++ b/solution.py
@@ -382,9 +382,11 @@
             return carry
 
         lax.fori_loop(0, levs, join, 0)
-        for p in lev_peers:
-            out_copy(c, p).start()
         own_out(c).start()
+        for p in range(levs):
+            @pl.when(p != d)
+            def _():
+                out_copy(c, p).start()
 
     gather_edges(0)
     start_in(2)

time: 50.7 us -> 50.7 us (level)
  no operation moved by 1% of the time
where the time goes in v4:
time: 50.7 us; the launch traced here: 50.1 us
  Pallas kernels  49.1 us (97%)
  local copies, waits for them, and re-layouts  0.97 us (2%)
    pallas_call x1, Pallas kernels, window(): pl.pallas_call(functools.partial(window_kernel, tiles, levs, members), ou...  49.1 us

profile of v4, /device:TPU:1, one launch (start us, length us, event | category | flops | bytes accessed | tf_op | source)
XLA Modules:
  0.0 50.1 jit_solution(14174330782206559421)
XLA Ops:
  0.0 49.1 %window.1 = f32[4,16,32,128]{3,2,1,0:T(8,128)S(1)} custom-call(f32[4,16]{1,0:T(4,128)} %rate_hbm.1, s32[4]{0:T(128)} %top_hbm.1, f32[4,16]{1,0:T(4,128)} %bitcast.12, s32[4,8]{1,0:T(4,128)} %bitcast.13, f32[4,16,32,128]{3,2,1,0:T(8,128)} %bitcast.8, f32[32,128]{1,0:T(8,128)} %bitcast.9, f32[32,128]{1,0:T(8,128)} %bitcast.10, f32[32,128]{1,0:T(8,128)} %bitcast.11), custom_call_target="tpu_custom_call" | custom-call | tf_op jit(solution)/shard_map/window/pallas_call | solution.py:428
  49.1 1.0 %copy.11 = f32[1,4,16,1,4096]{4,3,2,1,0:T(1,128)} copy(f32[1,4,16,1,4096]{4,3,2,1,0:T(1,128)S(1)} %bitcast.7) | data formatting | bytes 2097152
